TPU v7x, 32 devices: a whole 2x2x4 slice. The times are simulated.
32 devices in a mesh: seq: 8 (over z, y), dp: 4 (over x, core).
Axes of the slice: x: 2, y: 2, z: 4, core: 2. Of those that a mesh axis runs over, the one named last changes fastest.
Arguments:
- inputs: bfloat16 [4, 2048, 324], P('dp', 'seq'), may hold values from -6 to 6
- w_qkv: bfloat16 [324, 972], replicated, may hold values from -0.3125 to 0.3125
- w_pos: bfloat16 [324, 324], replicated, may hold values from -0.625 to 0.625
- w_out: bfloat16 [324, 324], replicated, may hold values from -1.25 to 1.25
- rel_bias: float32 [2, 324], replicated, may hold values from -3 to 3
- ffn_in: bfloat16 [2, 324, 1296], replicated, may hold values from -0.3125 to 0.3125
- ffn_out: bfloat16 [2, 1296, 324], replicated, may hold values from -0.15625 to 0.15625
- conv_in: bfloat16 [324, 648], replicated, may hold values from -0.3125 to 0.3125
- conv_depth: float32 [31, 324], replicated, may hold values from -1 to 1
- conv_out: bfloat16 [324, 324], replicated, may hold values from -0.3125 to 0.3125
- bn_gain: float32 [324], replicated, may hold values from 0.5 to 1.5
- bn_bias: float32 [324], replicated, may hold values from -2 to 2
- norm_gain: float32 [4, 324], replicated, may hold values from 0.5 to 1.5
- norm_bias: float32 [4, 324], replicated, may hold values from -2 to 2
- lengths: int32 [4, 8], P('dp'), may hold values from 1 to 1920, as said below
- cotangent: float32 [4, 2048, 324], P('dp', 'seq'), may hold values from -6 to 6
Outputs:
- layer_out: float32 [4, 2048, 324], P('dp', 'seq')
- input_grad: float32 [4, 2048, 324], P('dp', 'seq')
- grad_w_qkv: float32 [324, 972], replicated
- grad_w_pos: float32 [324, 324], replicated
- grad_w_out: float32 [324, 324], replicated
- grad_rel_bias: float32 [2, 324], replicated
- grad_ffn_in: float32 [2, 324, 1296], replicated
- grad_ffn_out: float32 [2, 1296, 324], replicated
- grad_conv_in: float32 [324, 648], replicated
- grad_conv_depth: float32 [31, 324], replicated
- grad_conv_out: float32 [324, 324], replicated
- grad_bn_gain: float32 [324], replicated
- grad_bn_bias: float32 [324], replicated
- grad_norm_gain: float32 [4, 324], replicated
- grad_norm_bias: float32 [4, 324], replicated
Inputs may be any that keep to these rules, and one draw needn't show every extreme that they name: `lengths`: in each stream one clip has exactly 1920 frames and starts within the first 128 frames; every other clip has at most 16 frames, and the one after the longest (cyclically) has 1; all clips together leave 1 to 127 unused frames at the end of the stream.
All inputs are finite; a program needn't handle non-finite values.
Results may differ from a plain program's by a relative error of at most 0.02.
Values may be sent and summed in bfloat16 or wider, within the bound.
No kernel may reach another device: no remote copies, remote signals or barrier semaphores. Data moves between devices by JAX's collectives and lax.ppermute only.
A program may use at most 192 MiB of HBM per device.

v0:
```python
import math

import jax
import jax.numpy as jnp
from jax import lax
from jax.sharding import PartitionSpec as P

HEADS = 4


def with_halo(block, sides, width):
    for axis, dim in sides:
        count = lax.axis_size(axis)
        forward = [(i, i + 1) for i in range(count - 1)]
        backward = [(target, source) for source, target in forward]
        low = lax.ppermute(
            lax.slice_in_dim(block, block.shape[dim] - width, None, axis=dim), axis, forward
        )
        high = lax.ppermute(lax.slice_in_dim(block, 0, width, axis=dim), axis, backward)
        block = jnp.concatenate([low, block, high], axis=dim)
    return block


def layer_norm(summed, gain_row, bias_row):
    average = jnp.mean(summed, axis=-1, keepdims=True)
    centered = summed - average
    variance = jnp.mean(centered * centered, axis=-1, keepdims=True)
    return centered * lax.rsqrt(variance + 1e-05) * gain_row + bias_row


def norm_back(summed, gain_row, bias_row, incoming):
    return jax.vjp(layer_norm, summed, gain_row, bias_row)[1](incoming)


def frame_tables(positions, model_width):
    frequency = jnp.exp(
        jnp.arange(model_width // 2, dtype=jnp.float32) * (-2.0 * math.log(10000.0) / model_width)
    )
    angles = positions.astype(jnp.float32)[:, None] * frequency[None, :]
    return (jnp.sin(angles), jnp.cos(angles))


def clip_of(positions, clip_ends):
    return jnp.sum((positions[:, None] >= clip_ends[None, :]).astype(jnp.int32), axis=1)


def rotate(shifted, sines, cosines):
    half_width = shifted.shape[-1] // 2
    first_half = shifted[..., :half_width]
    second_half = shifted[..., half_width:]
    return jnp.concatenate(
        [first_half * sines + second_half * cosines, second_half * sines - first_half * cosines],
        axis=-1,
    )


def plain_product(left, right):
    return jnp.dot(left, right, preferred_element_type=jnp.float32)


def times_transposed(left, right):
    return lax.dot_general(
        left, right, (((1,), (1,)), ((), ())), preferred_element_type=jnp.float32
    )


def transposed_times(left, right):
    return lax.dot_general(
        left, right, (((0,), (0,)), ((), ())), preferred_element_type=jnp.float32
    )


def gated_half(projected):
    half_width = projected.shape[1] // 2
    return projected[:, :half_width] * jax.nn.sigmoid(projected[:, half_width:])


def feed_forward(hidden_low, weight_in, weight_out):
    inner = plain_product(hidden_low, weight_in)
    activated = jax.nn.silu(inner).astype(jnp.bfloat16)
    return (inner, activated, plain_product(activated, weight_out))


def feed_back(hidden_low, inner, activated, weight_in, weight_out, incoming):
    incoming_low = incoming.astype(jnp.bfloat16)
    grad_out = transposed_times(activated, incoming_low)
    grad_act = times_transposed(incoming_low, weight_out)
    grad_inner = jax.vjp(jax.nn.silu, inner)[1](grad_act)[0].astype(jnp.bfloat16)
    grad_in = transposed_times(hidden_low, grad_inner)
    return (times_transposed(grad_inner, weight_in), grad_in, grad_out)


def block_scores(query_unit, query_pos, key_block, table_block, same_clip):
    raw = jnp.einsum("qhd,khd->hqk", query_unit, key_block, preferred_element_type=jnp.float32)
    raw = raw + jnp.einsum(
        "qhc,kc->hqk", query_pos, table_block, preferred_element_type=jnp.float32
    )
    return jnp.where(same_clip[None], raw / math.sqrt(query_unit.shape[2]), -1e30)


def block_rows(shard_rows, shard_count):
    parts = max(1, 512 // shard_rows)
    while shard_count % parts != 0:
        parts = parts - 1
    return shard_rows * parts


def local(
    inputs,
    w_qkv,
    w_pos,
    w_out,
    rel_bias,
    ffn_in,
    ffn_out,
    conv_in,
    conv_depth,
    conv_out,
    bn_gain,
    bn_bias,
    norm_gain,
    norm_bias,
    lengths,
    cotangent,
):
    input_low = inputs[0]
    input_float = input_low.astype(jnp.float32)
    frame_rows, model_width = input_low.shape
    head_count = HEADS
    head_width = model_width // head_count
    shard_count = lax.axis_size("seq")
    total_frames = frame_rows * shard_count
    first_frame = lax.axis_index("seq") * frame_rows
    clip_ends = jnp.cumsum(lengths[0])
    local_frames = first_frame + jnp.arange(frame_rows, dtype=jnp.int32)
    local_clip = clip_of(local_frames, clip_ends)
    valid_rows = (local_frames < clip_ends[-1]).astype(jnp.float32)[:, None]
    all_frames = jnp.arange(total_frames, dtype=jnp.int32)
    key_span = block_rows(frame_rows, shard_count)
    block_count = total_frames // key_span
    key_clip = clip_of(all_frames, clip_ends).reshape(block_count, key_span)
    all_sines, all_cosines = frame_tables(all_frames, model_width)
    key_table = (
        jnp.concatenate([all_cosines, all_sines], axis=1)
        .astype(jnp.bfloat16)
        .reshape(block_count, key_span, model_width)
    )
    local_sines, local_cosines = frame_tables(local_frames, model_width)

    def rotate_local(grid):
        return rotate(grid, local_sines[:, None, :], local_cosines[:, None, :])

    def split_keys(array):
        return array.reshape(block_count, key_span, head_count, head_width)

    projected = plain_product(input_low, w_qkv)
    query_part = projected[:, :model_width]
    key_low = projected[:, model_width : 2 * model_width].astype(jnp.bfloat16)
    value_low = projected[:, 2 * model_width :].astype(jnp.bfloat16)
    query_unit = (
        (query_part + rel_bias[0]).astype(jnp.bfloat16).reshape(frame_rows, head_count, head_width)
    )
    query_shift = (
        (query_part + rel_bias[1]).astype(jnp.bfloat16).reshape(frame_rows, head_count, head_width)
    )
    pos_grid = w_pos.reshape(model_width, head_count, head_width)
    shifted = jnp.einsum("fhd,chd->fhc", query_shift, pos_grid, preferred_element_type=jnp.float32)
    query_pos = rotate_local(shifted).astype(jnp.bfloat16)
    keys_all, values_all = (
        lax.all_gather(key_low, "seq", axis=0, tiled=True),
        lax.all_gather(value_low, "seq", axis=0, tiled=True),
    )

    def scores_of(key_block, table_block, clip_block):
        same_clip = local_clip[:, None] == clip_block[None, :]
        return block_scores(query_unit, query_pos, key_block, table_block, same_clip)

    def norm_step(carry, pieces):
        highest, total = carry
        key_block, table_block, clip_block = pieces
        scores = scores_of(key_block, table_block, clip_block)
        new_highest = jnp.maximum(highest, jnp.max(scores, axis=2))
        total = total * jnp.exp(highest - new_highest) + jnp.sum(
            jnp.exp(scores - new_highest[..., None]), axis=2
        )
        return ((new_highest, total), None)

    start_carry = (
        jnp.full((head_count, frame_rows), -1e30, jnp.float32),
        jnp.zeros((head_count, frame_rows), jnp.float32),
    )
    (highest, total), _ = lax.scan(
        norm_step, start_carry, (split_keys(keys_all), key_table, key_clip)
    )
    log_total = highest + jnp.log(total)

    def value_step(summed, pieces):
        key_block, value_block, table_block, clip_block = pieces
        weights = jnp.exp(
            scores_of(key_block, table_block, clip_block) - log_total[..., None]
        ).astype(jnp.bfloat16)
        return (
            summed
            + jnp.einsum("hqk,khd->qhd", weights, value_block, preferred_element_type=jnp.float32),
            None,
        )

    attended, _ = lax.scan(
        value_step,
        jnp.zeros((frame_rows, head_count, head_width), jnp.float32),
        (split_keys(keys_all), split_keys(values_all), key_table, key_clip),
    )
    attended_low = attended.reshape(frame_rows, model_width).astype(jnp.bfloat16)
    first_sum = input_float + plain_product(attended_low, w_out)
    first_norm = layer_norm(first_sum, norm_gain[0], norm_bias[0])
    first_low = first_norm.astype(jnp.bfloat16)
    inner_early, act_early, out_early = feed_forward(first_low, ffn_in[0], ffn_out[0])
    second_sum = first_norm + out_early
    second_norm = layer_norm(second_sum, norm_gain[1], norm_bias[1])
    second_low = second_norm.astype(jnp.bfloat16)
    gate_values = plain_product(second_low, conv_in)
    gated = gated_half(gate_values).astype(jnp.bfloat16)
    reach = conv_depth.shape[0] // 2
    ext_clip = clip_of(
        first_frame - reach + jnp.arange(frame_rows + 2 * reach, dtype=jnp.int32), clip_ends
    )
    gated_ext = with_halo(gated, (("seq", 0),), reach)
    convolved = jnp.zeros((frame_rows, model_width), jnp.float32)
    for offset in range(2 * reach + 1):
        same_clip = (ext_clip[offset : offset + frame_rows] == local_clip)[:, None]
        convolved = convolved + conv_depth[offset] * jnp.where(
            same_clip, gated_ext[offset : offset + frame_rows].astype(jnp.float32), 0.0
        )
    frame_count, first_moment, second_moment = lax.psum(
        (
            jnp.sum(valid_rows),
            jnp.sum(convolved * valid_rows, axis=0),
            jnp.sum(convolved * convolved * valid_rows, axis=0),
        ),
        ("seq", "dp"),
    )
    batch_mean = first_moment / frame_count
    batch_var = second_moment / frame_count - batch_mean * batch_mean
    inverse_std = lax.rsqrt(batch_var + 1e-05)
    centered_conv = (convolved - batch_mean) * inverse_std
    normed = centered_conv * bn_gain + bn_bias
    swished = jax.nn.silu(normed).astype(jnp.bfloat16)
    third_sum = second_norm + plain_product(swished, conv_out)
    third_norm = layer_norm(third_sum, norm_gain[2], norm_bias[2])
    third_low = third_norm.astype(jnp.bfloat16)
    inner_late, act_late, out_late = feed_forward(third_low, ffn_in[1], ffn_out[1])
    fourth_sum = third_norm + out_late
    result = layer_norm(fourth_sum, norm_gain[3], norm_bias[3])
    grad_fourth, gain_three, bias_three = norm_back(
        fourth_sum, norm_gain[3], norm_bias[3], cotangent[0]
    )
    from_late, d_in_late, d_out_late = feed_back(
        third_low, inner_late, act_late, ffn_in[1], ffn_out[1], grad_fourth
    )
    grad_third, gain_two, bias_two = norm_back(
        third_sum, norm_gain[2], norm_bias[2], grad_fourth + from_late
    )
    third_grad_low = grad_third.astype(jnp.bfloat16)
    d_conv_out = transposed_times(swished, third_grad_low)
    d_swished = times_transposed(third_grad_low, conv_out)
    d_normed = jax.vjp(jax.nn.silu, normed)[1](d_swished)[0]
    scaled = d_normed * bn_gain
    d_bn_gain, d_bn_bias, sum_scaled, sum_product = lax.psum(
        (
            jnp.sum(d_normed * centered_conv, axis=0),
            jnp.sum(d_normed, axis=0),
            jnp.sum(scaled, axis=0),
            jnp.sum(scaled * centered_conv, axis=0),
        ),
        ("seq", "dp"),
    )
    d_conv = (
        inverse_std
        * (scaled - valid_rows * (sum_scaled + centered_conv * sum_product) / frame_count)
    ).astype(jnp.bfloat16)
    d_conv_ext = with_halo(d_conv, (("seq", 0),), reach)
    d_conv_float = d_conv.astype(jnp.float32)
    d_gated = jnp.zeros((frame_rows, model_width), jnp.float32)
    depth_terms = []
    for offset in range(2 * reach + 1):
        same_clip = (ext_clip[offset : offset + frame_rows] == local_clip)[:, None]
        depth_terms.append(
            jnp.sum(
                jnp.where(
                    same_clip, gated_ext[offset : offset + frame_rows].astype(jnp.float32), 0.0
                )
                * d_conv_float,
                axis=0,
            )
        )
        mirror = 2 * reach - offset
        mirror_clip = (ext_clip[mirror : mirror + frame_rows] == local_clip)[:, None]
        d_gated = d_gated + conv_depth[offset] * jnp.where(
            mirror_clip, d_conv_ext[mirror : mirror + frame_rows].astype(jnp.float32), 0.0
        )
    d_depth = jnp.stack(depth_terms)
    d_gates = jax.vjp(gated_half, gate_values)[1](d_gated)[0].astype(jnp.bfloat16)
    d_conv_in = transposed_times(second_low, d_gates)
    grad_second, gain_one, bias_one = norm_back(
        second_sum, norm_gain[1], norm_bias[1], grad_third + times_transposed(d_gates, conv_in)
    )
    late_terms = (d_in_late, d_out_late, d_conv_in, d_depth, d_conv_out)
    from_early, d_in_early, d_out_early = feed_back(
        first_low, inner_early, act_early, ffn_in[0], ffn_out[0], grad_second
    )
    grad_first, gain_zero, bias_zero = norm_back(
        first_sum, norm_gain[0], norm_bias[0], grad_second + from_early
    )
    first_grad_low = grad_first.astype(jnp.bfloat16)
    d_w_out = transposed_times(attended_low, first_grad_low)
    d_attended = (
        times_transposed(first_grad_low, w_out)
        .astype(jnp.bfloat16)
        .reshape(frame_rows, head_count, head_width)
    )
    keys_back, values_back = (keys_all, values_all)

    def delta_step(summed, pieces):
        key_block, value_block, table_block, clip_block = pieces
        probs = jnp.exp(scores_of(key_block, table_block, clip_block) - log_total[..., None])
        slope = jnp.einsum(
            "qhd,khd->hqk", d_attended, value_block, preferred_element_type=jnp.float32
        )
        return (summed + jnp.sum(probs * slope, axis=2), None)

    key_pieces = (split_keys(keys_back), split_keys(values_back), key_table, key_clip)
    delta, _ = lax.scan(delta_step, jnp.zeros((head_count, frame_rows), jnp.float32), key_pieces)

    def grad_step(carry, pieces):
        d_unit, d_pos = carry
        key_block, value_block, table_block, clip_block = pieces
        probs = jnp.exp(scores_of(key_block, table_block, clip_block) - log_total[..., None])
        slope = jnp.einsum(
            "qhd,khd->hqk", d_attended, value_block, preferred_element_type=jnp.float32
        )
        d_raw = (probs * (slope - delta[..., None]) / math.sqrt(head_width)).astype(jnp.bfloat16)
        d_value = jnp.einsum(
            "hqk,qhd->khd",
            probs.astype(jnp.bfloat16),
            d_attended,
            preferred_element_type=jnp.float32,
        )
        d_key = jnp.einsum("hqk,qhd->khd", d_raw, query_unit, preferred_element_type=jnp.float32)
        d_unit = d_unit + jnp.einsum(
            "hqk,khd->qhd", d_raw, key_block, preferred_element_type=jnp.float32
        )
        d_pos = d_pos + jnp.einsum(
            "hqk,kc->qhc", d_raw, table_block, preferred_element_type=jnp.float32
        )
        return ((d_unit, d_pos), (d_key, d_value))

    start_grads = (
        jnp.zeros((frame_rows, head_count, head_width), jnp.float32),
        jnp.zeros((frame_rows, head_count, model_width), jnp.float32),
    )
    (d_unit, d_pos), (key_blocks, value_blocks) = lax.scan(grad_step, start_grads, key_pieces)
    d_keys, d_values = (
        lax.psum_scatter(
            key_blocks.reshape(total_frames, model_width).astype(jnp.bfloat16),
            "seq",
            scatter_dimension=0,
            tiled=True,
        ).astype(jnp.float32),
        lax.psum_scatter(
            value_blocks.reshape(total_frames, model_width).astype(jnp.bfloat16),
            "seq",
            scatter_dimension=0,
            tiled=True,
        ).astype(jnp.float32),
    )
    d_shifted = jax.vjp(rotate_local, shifted)[1](d_pos)[0].astype(jnp.bfloat16)
    d_w_pos = jnp.einsum(
        "fhc,fhd->chd", d_shifted, query_shift, preferred_element_type=jnp.float32
    ).reshape(model_width, model_width)
    d_from_pos = jnp.einsum("fhc,chd->fhd", d_shifted, pos_grid, preferred_element_type=jnp.float32)
    d_rel = jnp.stack(
        [
            jnp.sum(d_unit, axis=0).reshape(model_width),
            jnp.sum(d_from_pos, axis=0).reshape(model_width),
        ]
    )
    d_query = (d_unit + d_from_pos).reshape(frame_rows, model_width)
    d_proj = jnp.concatenate([d_query, d_keys, d_values], axis=1).astype(jnp.bfloat16)
    d_w_qkv = transposed_times(input_low, d_proj)
    input_grad = grad_first + times_transposed(d_proj, w_qkv)
    gain_grads = jnp.stack([gain_zero, gain_one, gain_two, gain_three])
    bias_grads = jnp.stack([bias_zero, bias_one, bias_two, bias_three])
    summed_all = lax.psum(
        (
            d_w_qkv,
            d_w_pos,
            d_w_out,
            d_rel,
            d_in_early,
            d_out_early,
            gain_grads,
            bias_grads,
            d_in_late,
            d_out_late,
            d_conv_in,
            d_depth,
            d_conv_out,
        ),
        ("seq", "dp"),
    )
    early_terms = summed_all[:8]
    late_terms = summed_all[8:]
    sum_qkv, sum_pos, sum_wout, sum_rel, sum_in_early, sum_out_early, sum_gain, sum_bias = (
        early_terms
    )
    sum_in_late, sum_out_late, sum_conv_in, sum_depth, sum_conv_out = late_terms
    return (
        result[None],
        input_grad[None],
        sum_qkv,
        sum_pos,
        sum_wout,
        sum_rel,
        jnp.stack([sum_in_early, sum_in_late]),
        jnp.stack([sum_out_early, sum_out_late]),
        sum_conv_in,
        sum_depth,
        sum_conv_out,
        d_bn_gain,
        d_bn_bias,
        sum_gain,
        sum_bias,
    )


def solution(mesh):
    placed = (
        P("dp", "seq", None),
        P(),
        P(),
        P(),
        P(),
        P(),
        P(),
        P(),
        P(),
        P(),
        P(),
        P(),
        P(),
        P(),
        P("dp", None),
        P("dp", "seq", None),
    )
    return jax.shard_map(
        local,
        mesh=mesh,
        in_specs=placed,
        out_specs=(
            P("dp", "seq", None),
            P("dp", "seq", None),
            P(),
            P(),
            P(),
            P(),
            P(),
            P(),
            P(),
            P(),
            P(),
            P(),
            P(),
            P(),
            P(),
        ),
        check_vma=False,
    )
```

profile of v0, /device:TPU:0, one launch (start us, length us, event | category | flops | bytes accessed | tf_op | source)
XLA Modules:
  0.0 784.9 jit_solution(9740512089973416639)
XLA Ops:
  12.3 5.5 fusion.79
  26.1 4.3 fusion.240
  30.5 4.3 fusion.239
  34.8 21.3 %all-gather.3.cloned.1.call-done = bf16[2048,324]{0,1:T(8,128)(2,1)} async-done(((bf16[256,324]{0,1:T(8,128)(2,1)}), bf16[2048,324]{0,1:T(8,128)(2,1)}) %all-gather.3.cloned.1.call-update) | async-done | bytes 1327120 | tf_op jit(solution)/shard_map/all_gather | solution.py:171
  56.0 3.3 reshape.457
  60.7 39.2 %all-gather.5.cloned.1.call-done = bf16[2048,324]{0,1:T(8,128)(2,1)} async-done(((bf16[256,324]{0,1:T(8,128)(2,1)}), bf16[2048,324]{0,1:T(8,128)(2,1)}) %all-gather.5.cloned.1.call-update) | async-done | bytes 1327120 | tf_op jit(solution)/shard_map/all_gather | solution.py:170
  99.9 3.3 reshape.460
  104.6 19.3 %while.52 = (s32[]{:T(128)}, f32[4,256]{1,0:T(4,128)S(1)}, f32[4,256]{1,0:T(4,128)S(1)}, s32[256]{0:T(256)S(1)}, s32[4,512]{1,0:T(4,128)}, /*index=5*/bf16[4,512...) while((s32[]{:T(128)}, f32[4,256]{1,0:T(4,128)S(1)}, ...), condition=%wide.region_6.7_spmd.clone, body=%wide.region_3.6_spmd.clone.sunk | while | flops 427955200 | bytes 10245260 | solution.py:192
  124.5 23.0 %while.53 = (s32[]{:T(128)}, f32[256,4,81]{0,2,1:T(8,128)}, bf16[4,512,4,81]{1,3,2,0:T(8,128)(2,1)}, s32[256]{0:T(256)S(1)}, s32[4,512]{1,0:T(4,128)}, /*index=5...) while((s32[]{:T(128)}, f32[256,4,81]{0,2,1:T(8,128)}, ...), condition=%wide.region_8.9_spmd.clone, body=%wide.region_7.8_spmd.clone.sunk | while | flops 512526336 | bytes 7056014 | solution.py:208
  126.9 3.3 fusion.338
  132.5 3.4 fusion.338
  138.3 3.4 fusion.338
  144.1 3.4 fusion.338
  154.9 4.6 collective-permute-start
  162.2 6.4 multiply_reduce_fusion.12
  168.7 42.1 %all-reduce.6 = (f32[324]{0:T(512)S(1)}, f32[]{:T(128)}, f32[324]{0:T(512)S(1)}) all-reduce(f32[324]{0:T(512)S(1)} %get-tuple-element.629, f32[]{:T(128)} %fusion.224, f32[324]{0:T(512)S(1)} %get-tuple-element.628), channel_id=1, replica_groups=mesh['seq'=8,'dp'=4] {'seq','dp'}, use_global_device_ids=true, to_apply=%region_19.20 | all-reduce | flops 649 | bytes 5192 | tf_op jit(solution)/shard_map/psum | solution.py:234
  222.2 39.7 %all-reduce.5 = (f32[324]{0:T(512)}, f32[324]{0:T(512)}) all-reduce(f32[324]{0:T(512)S(1)} %get-tuple-element.588, f32[324]{0:T(512)S(1)} %get-tuple-element.627), channel_id=1, replica_groups=mesh['seq'=8,'dp'=4] {'seq','dp'}, use_global_device_ids=true, to_apply=%region_31.32 | all-reduce | flops 648 | bytes 5184 | tf_op jit(solution)/shard_map/psum | solution.py:268
  261.9 3.3 fusion.141
  266.0 4.6 collective-permute-start.3
  272.9 4.3 collective-permute-done.2
  277.2 9.4 %fusion.94 = (f32[256,324]{0,1:T(8,128)S(1)}, f32[256,324]{0,1:T(8,128)S(1)}) fusion(f32[256,648]{0,1:T(8,128)S(1)} %fusion.228, bf16[256,324]{0,1:T(8,128)(2,1)S(1)} %get-tuple-element.786, bf16[15,324]{0,1:T(8,128)(2,1)S(1)} %collective-permute-done.3, pred[256]{0:T(512)(128)(4,1)} %get-tuple-element.822, f32[324]{0:T(512)} %copy-done.123, ...), kind=kLoop, calls=%fused_computation.304 | loop fusion | flops 18247680 | bytes 1560544 | tf_op jit(solution)/shard_map/transpose(jvp())/mul | solution.py:75
  293.0 29.0 %while.54 = (s32[]{:T(128)}, f32[4,256]{1,0:T(4,128)}, s32[256]{0:T(256)S(1)}, s32[4,512]{1,0:T(4,128)}, bf16[4,512,4,81]{1,3,2,0:T(8,128)(2,1)}, /*index=5*/bf1...) while((s32[]{:T(128)}, f32[4,256]{1,0:T(4,128)}, ...), condition=%wide.region_38.39_spmd.clone, body=%wide.region_36.38_spmd.clone.sunk | while | flops 512885760 | bytes 10738847 | solution.py:332
  321.9 62.0 %while.55 = (s32[]{:T(128)}, f32[256,4,81]{0,2,1:T(8,128)}, f32[256,4,324]{0,2,1:T(8,128)}, bf16[4,512,4,81]{1,3,2,0:T(8,128)(2,1)}, bf16[4,512,4,81]{1,3,2,0:T(...) while((s32[]{:T(128)}, f32[256,4,81]{0,2,1:T(8,128)}, ...), condition=%wide.region_40.41_spmd.clone, body=%wide.region_39.40_spmd.clone.sunk | while | flops 1109829632 | bytes 48307548 | solution.py:361
  346.6 3.1 fusion.366
  362.2 3.1 fusion.366
  377.8 3.1 fusion.366
  408.5 41.1 %reduce-scatter.5.cloned.1.call-done = bf16[256,324]{0,1:T(8,128)(2,1)} async-done(((bf16[2048,324]{0,1:T(8,128)(2,1)}), bf16[256,324]{0,1:T(8,128)(2,1)}) %reduce-scatter.5.cloned.1.call-update) | async-done | bytes 165904 | tf_op jit(solution)/shard_map/reduce_scatter | solution.py:369
  449.6 63.8 %reduce-scatter.3.cloned.1.call-done = bf16[256,324]{0,1:T(8,128)(2,1)} async-done(((bf16[2048,324]{0,1:T(8,128)(2,1)}), bf16[256,324]{0,1:T(8,128)(2,1)}) %reduce-scatter.3.cloned.1.call-update) | async-done | bytes 165904 | tf_op jit(solution)/shard_map/reduce_scatter | solution.py:363
  524.3 42.1 %all-reduce.4 = (f32[2,324]{1,0:T(2,128)}, f32[31,324]{1,0:T(8,128)}, f32[324]{0:T(512)}, f32[324]{0:T(512)}, f32[4,324]{1,0:T(4,128)}, /*index=5*/f32[4,324]{1,0:T(4,128)}) all-reduce(f32[2,324]{1,0:T(2,128)S(1)} %pad_maximum_fusion.13, f32[31,324]{1,0:T(8,128)S(1)} %stack.169, ...), channel_id=1, replica_groups=mesh['seq'=8,'dp'=4] {'seq','dp'}, use_global_device_ids=true, to_apply=%region_48.49 | all-reduce | flops 13932 | bytes 111456 | tf_op jit(solution)/shard_map/psum | solution.py:393
  567.9 194.2 %all-reduce.10.cloned.1.call-done = (f32[324,972]{1,0:T(8,128)}, f32[324,324]{0,1:T(8,128)}, f32[324,324]{1,0:T(8,128)}, f32[1,324,1296]{2,1,0:T(8,128)}, f32[1,...) async-done(((f32[324,972]{1,0:T(8,128)}, f32[324,324]{0,1:T(8,128)}, ...) | async-done | bytes 10077712 | tf_op jit(solution)/shard_map/psum | solution.py:393
  766.4 3.7 copy.100
  770.4 3.7 copy.101
  (762 shorter events, 199.4 us)
Async XLA Ops:
  7.2 48.8 %all-gather.3.cloned.1.call-start = ((), (), s32[]{:S(2)}) async-start(), calls=%async_computation.2 | async-start | bytes 1511424 | tf_op jit(solution)/shard_map/all_gather | solution.py:171
  10.5 89.5 %all-gather.5.cloned.1.call-start = ((), (), s32[]{:S(2)}) async-start(), calls=%async_computation.3 | async-start | bytes 1511424 | tf_op jit(solution)/shard_map/all_gather | solution.py:170
  11.2 438.4 %reduce-scatter.5.cloned.1.call-start = ((), (), s32[]{:S(2)}) async-start(), calls=%async_computation.5 | async-start | bytes 1511424 | tf_op jit(solution)/shard_map/reduce_scatter | solution.py:369
  20.3 130.6 %copy-start.81 = (f32[324]{0:T(512)}, f32[324]{0:T(512)S(1)}, u32[]{:S(2)}) copy-start(f32[324]{0:T(512)S(1)} %get-tuple-element.873) | copy-start | bytes 3892
  20.3 130.7 %copy-start.128 = (f32[324]{0:T(512)}, f32[324]{0:T(512)S(1)}, u32[]{:S(2)}) copy-start(f32[324]{0:T(512)S(1)} %get-tuple-element.672) | copy-start | bytes 3892
  20.3 132.5 %copy-start.75 = (f32[324]{0:T(512)}, f32[324]{0:T(512)S(1)}, u32[]{:S(2)}) copy-start(f32[324]{0:T(512)S(1)} %get-tuple-element.874) | copy-start | bytes 3892
  20.3 132.5 %copy-start.125 = (f32[324]{0:T(512)}, f32[324]{0:T(512)S(1)}, u32[]{:S(2)}) copy-start(f32[324]{0:T(512)S(1)} %get-tuple-element.671) | copy-start | bytes 3892
  124.5 24.2 %copy-start.37 = (bf16[1,256,324]{1,2,0:T(8,128)(2,1)S(1)}, bf16[1,256,324]{1,2,0:T(8,128)(2,1)}, u32[]{:S(2)}) copy-start(bf16[1,256,324]{1,2,0:T(8,128)(2,1)} %param.24) | copy-start | bytes 497668
  150.0 141.8 %copy-start.4 = (f32[256,324]{0,1:T(8,128)}, f32[256,324]{0,1:T(8,128)S(1)}, u32[]{:S(2)}) copy-start(f32[256,324]{0,1:T(8,128)S(1)} %get-tuple-element.860) | copy-start | bytes 995332
  150.1 141.8 %copy-start.86 = (f32[256]{0:T(256)}, f32[256]{0:T(256)S(1)}, u32[]{:S(2)}) copy-start(f32[256]{0:T(256)S(1)} %broadcast_multiply_fusion.3) | copy-start | bytes 3076
  152.4 136.4 %copy-start.6 = (f32[256,324]{0,1:T(8,128)}, f32[256,324]{0,1:T(8,128)S(1)}, u32[]{:S(2)}) copy-start(f32[256,324]{0,1:T(8,128)S(1)} %get-tuple-element.862) | copy-start | bytes 995332
  152.4 136.4 %copy-start.79 = (f32[256]{0:T(256)}, f32[256]{0:T(256)S(1)}, u32[]{:S(2)}) copy-start(f32[256]{0:T(256)S(1)} %broadcast_multiply_fusion.2) | copy-start | bytes 3076
  152.5 9.3 %copy-start.93 = (f32[324]{0:T(512)S(1)}, f32[324]{0:T(512)}, u32[]{:S(2)}) copy-start(f32[324]{0:T(512)} %get-tuple-element.635) | copy-start | bytes 3892
  152.8 58.6 %copy-start.90 = (f32[256]{0:T(256)}, f32[256]{0:T(256)S(1)}, u32[]{:S(2)}) copy-start(f32[256]{0:T(256)S(1)} %fusion.215) | copy-start | bytes 3076
  153.4 58.1 %copy-start.76 = (f32[324]{0:T(512)S(1)}, f32[324]{0:T(512)}, u32[]{:S(2)}) copy-start(f32[324]{0:T(512)} %copy-done.75) | copy-start | bytes 3892
  153.4 58.1 %copy-start.126 = (f32[324]{0:T(512)S(1)}, f32[324]{0:T(512)}, u32[]{:S(2)}) copy-start(f32[324]{0:T(512)} %copy-done.125) | copy-start | bytes 3892
  153.6 8.2 %collective-permute-start.1 = (bf16[15,324]{0,1:T(8,128)(2,1)S(1)}, bf16[15,324]{0,1:T(8,128)(2,1)S(1)}, u32[]{:S(2)}, u32[]{:S(2)}) collective-permute-start(bf16[15,324]{0,1:T(8,128)(2,1)S(1)} %get-tuple-element.819), channel_id=1, source_target_pairs={{4,0},{8,4},{12,8},{16,12},{20,16},{24,20},{28,24},{5,1},{9,5},{13... | collective-permute-start | bytes 29168 | tf_op jit(solution)/shard_map/ppermute | solution.py:19
  154.9 6.9 collective-permute-start
  161.8 100.1 %copy-start.50 = (bf16[15,324]{0,1:T(8,128)(2,1)}, bf16[15,324]{0,1:T(8,128)(2,1)S(1)}, u32[]{:S(2)}) copy-start(bf16[15,324]{0,1:T(8,128)(2,1)S(1)} %collective-permute-done.1) | copy-start | bytes 29164
  168.5 93.4 %copy-start.46 = (f32[256,324]{0,1:T(8,128)}, f32[256,324]{0,1:T(8,128)S(1)}, u32[]{:S(2)}) copy-start(f32[256,324]{0,1:T(8,128)S(1)} %get-tuple-element.797) | copy-start | bytes 995332
  220.6 41.4 %copy-start.145 = (f32[256]{0:T(256)S(1)}, f32[256]{0:T(256)}, u32[]{:S(2)}) copy-start(f32[256]{0:T(256)} %get-tuple-element.876) | copy-start | bytes 3076
  222.2 55.0 %copy-start.94 = (f32[324]{0:T(512)S(1)}, f32[324]{0:T(512)}, u32[]{:S(2)}) copy-start(f32[324]{0:T(512)} %get-tuple-element.635) | copy-start | bytes 3892
  266.0 20.8 %copy-start.53 = (f32[256,324]{0,1:T(8,128)S(1)}, f32[256,324]{0,1:T(8,128)}, u32[]{:S(2)}) copy-start(f32[256,324]{0,1:T(8,128)} %copy-done.52) | copy-start | bytes 995332
  266.0 20.8 %copy-start.91 = (f32[256]{0:T(256)S(1)}, f32[256]{0:T(256)}, u32[]{:S(2)}) copy-start(f32[256]{0:T(256)} %copy-done.90) | copy-start | bytes 3076
  266.0 6.9 collective-permute-start.3
  270.5 6.7 collective-permute-start.2
  388.3 125.1 %reduce-scatter.3.cloned.1.call-start = ((), (), s32[]{:S(2)}) async-start(), calls=%async_computation.4 | async-start | bytes 1511424 | tf_op jit(solution)/shard_map/reduce_scatter | solution.py:363
  391.7 370.3 %all-reduce.10.cloned.1.call-start = ((), (), s32[]{:S(2)}) async-start(), calls=%async_computation.6 | async-start | bytes 22478848 | tf_op jit(solution)/shard_map/psum | solution.py:393
  406.7 106.8 %copy-start.38 = (bf16[1,256,324]{1,2,0:T(8,128)(2,1)S(1)}, bf16[1,256,324]{1,2,0:T(8,128)(2,1)}, u32[]{:S(2)}) copy-start(bf16[1,256,324]{1,2,0:T(8,128)(2,1)} %param.24) | copy-start | bytes 497668
  406.7 106.8 %copy-start.62 = (bf16[256,324]{0,1:T(8,128)(2,1)S(1)}, bf16[256,324]{0,1:T(8,128)(2,1)}, u32[]{:S(2)}) copy-start(bf16[256,324]{0,1:T(8,128)(2,1)} %reshape.465) | copy-start | bytes 497668
  519.3 47.2 %copy-start.73 = (bf16[256,324]{0,1:T(8,128)(2,1)S(1)}, bf16[256,324]{0,1:T(8,128)(2,1)}, u32[]{:S(2)}) copy-start(bf16[256,324]{0,1:T(8,128)(2,1)} %reduce-scatter.5.cloned.1.call-done) | copy-start | bytes 497668
  519.3 47.2 %copy-start.74 = (bf16[256,324]{0,1:T(8,128)(2,1)S(1)}, bf16[256,324]{0,1:T(8,128)(2,1)}, u32[]{:S(2)}) copy-start(bf16[256,324]{0,1:T(8,128)(2,1)} %reduce-scatter.3.cloned.1.call-done) | copy-start | bytes 497668
  (216 other events, 926.8 us)
Sparse Core Ops, SparseCore 0:
  10.7 45.3 all-gather.2
  58.7 41.2 all-gather.4
  388.4 61.1 reduce-scatter.4
  452.9 60.4 reduce-scatter.2
  520.8 241.1 all-reduce.9
where the time goes:
time: 798 us; the launch traced here: 785 us
  waiting for transfers between devices  366 us (46%)
  matrix products  137 us (17%)
  blocking collectives  124 us (16%)
  local copies, waits for them, and re-layouts  75.6 us (9%)
  other arithmetic  52.3 us (7%)
  between operations  17.7 us (2%)
  starting transfers between devices  12.1 us (2%)
    psum x1, waiting for transfers between devices, local(): lax.psum((d_w_qkv, d_w_pos, d_w_out, d_rel, d_in_early, d_out_early, gain...  194 us
    reduce_scatter x1, waiting for transfers between devices, local(): lax.psum_scatter(key_blocks.reshape(total_frames, model_width).astype(jnp...  63.8 us
    psum x1, blocking collectives, local(): lax.psum((d_w_qkv, d_w_pos, d_w_out, d_rel, d_in_early, d_out_early, gain...  42.1 us
    psum x1, blocking collectives, local(): lax.psum((jnp.sum(valid_rows), jnp.sum(convolved * valid_rows, axis=0), j...  42.1 us
    reduce_scatter x1, waiting for transfers between devices, local(): lax.psum_scatter(value_blocks.reshape(total_frames, model_width).astype(j...  41.1 us
    psum x1, blocking collectives, local(): lax.psum((jnp.sum(d_normed * centered_conv, axis=0), jnp.sum(d_normed, ax...  39.7 us
    all_gather x1, waiting for transfers between devices, local(): lax.all_gather(key_low, 'seq', axis=0, tiled=True)  39.2 us
    unnamed x454, local copies, waits for them, and re-layouts  30.1 us
  transfers between devices with their start and end apart: 9, of which 7 were waited for; matrix products, arithmetic and copies ran while one was open for 7% of the time, Pallas kernels for 0%

commit v1 on v0

--- a/solution.py
+++ b/solution.py
@@ -6,6 +6,128 @@
 from jax.sharding import PartitionSpec as P
 
 HEADS = 4
+
+MODEL_AXES = ("seq", "dp")
+
+
+def device_count():
+    return lax.axis_size("seq") * lax.axis_size("dp")
+
+
+def flat_index():
+    return lax.axis_index("seq") * lax.axis_size("dp") + lax.axis_index("dp")
+
+
+def swap_flat(block, distance):
+    pairs = [(i, i ^ distance) for i in range(device_count())]
+    return lax.ppermute(block, MODEL_AXES, pairs)
+
+
+def swap_seq(block, distance):
+    pairs = [(i, i ^ distance) for i in range(lax.axis_size("seq"))]
+    return lax.ppermute(block, "seq", pairs)
+
+
+def pick(stacked, index):
+    return lax.dynamic_index_in_dim(stacked, index, 0, keepdims=False)
+
+
+def stage_radices(devices):
+    radices = [2]
+    left = devices // 2
+    while left > 1:
+        radix = 4 if left % 4 == 0 else 2
+        radices.append(radix)
+        left = left // radix
+    return radices
+
+
+def sum_everywhere(pieces):
+    devices, rows, width = pieces.shape
+    radices = stage_radices(devices)
+    place = flat_index()
+    held = pieces
+    strides = []
+    stride = 1
+    for radix in radices:
+        digit = (place // stride) % radix
+        held = held.reshape(radix, held.shape[0] // radix, rows, width)
+        total = pick(held, digit).astype(jnp.float32)
+        arrived = [
+            swap_flat(pick(held, digit ^ step), step * stride) for step in range(radix - 1, 0, -1)
+        ]
+        for part in arrived:
+            total = total + part.astype(jnp.float32)
+        held = total.astype(pieces.dtype)
+        strides.append(stride)
+        stride = stride * radix
+    for radix, stride in zip(radices[::-1], strides[::-1]):
+        digit = (place // stride) % radix
+        arrived = [held] + [swap_flat(held, step * stride) for step in range(1, radix)]
+        gathered = jnp.zeros((radix,) + held.shape, held.dtype)
+        for step in range(radix):
+            gathered = lax.dynamic_update_index_in_dim(gathered, arrived[step], digit ^ step, 0)
+        held = gathered.reshape(radix * held.shape[0], rows, width)
+    return held
+
+
+def sum_rows_everywhere(parts):
+    devices = device_count()
+    width = parts[0].shape[1]
+    rows = sum(part.shape[0] for part in parts)
+    share = -(-rows // (16 * devices)) * 16
+    padding = jnp.zeros((share * devices - rows, width), jnp.bfloat16)
+    packed = jnp.concatenate([part.astype(jnp.bfloat16) for part in parts] + [padding], axis=0)
+    summed = sum_everywhere(packed.reshape(devices, share, width)).reshape(share * devices, width)
+    result = []
+    start = 0
+    for part in parts:
+        result.append(summed[start : start + part.shape[0]].astype(jnp.float32))
+        start = start + part.shape[0]
+    return result
+
+
+def sum_small(rows_list):
+    flat = jnp.concatenate([jnp.ravel(row) for row in rows_list])
+    tiles = -(-flat.shape[0] // 1024)
+    tile = jnp.pad(flat, (0, tiles * 1024 - flat.shape[0])).reshape(tiles * 8, 128)
+    devices = device_count()
+    spread = jnp.broadcast_to(tile[None], (devices,) + tile.shape)
+    summed = jnp.sum(lax.all_to_all(spread, MODEL_AXES, 0, 0), axis=0).reshape(-1)
+    result = []
+    start = 0
+    for row in rows_list:
+        size = math.prod(row.shape)
+        result.append(summed[start : start + size].reshape(row.shape))
+        start = start + size
+    return result
+
+
+def gather_frames(shard):
+    count = lax.axis_size("seq")
+    across = [shard] + [swap_seq(shard, 2 * step) for step in range(1, count // 2)]
+    blocks = []
+    for block in across:
+        blocks.append(block)
+        blocks.append(swap_seq(block, 1))
+    return jnp.stack(blocks)
+
+
+def scatter_frames(partials):
+    count = lax.axis_size("seq")
+    total = None
+    for step in range(count // 2 - 1, -1, -1):
+        joined = partials[2 * step].astype(jnp.float32) + swap_seq(
+            partials[2 * step + 1], 1
+        ).astype(jnp.float32)
+        if step > 0:
+            joined = swap_seq(joined.astype(jnp.bfloat16), 2 * step).astype(jnp.float32)
+        total = joined if total is None else total + joined
+    return total
+
+
+def column_tiles(array, width):
+    return [array[:, start : start + width] for start in range(0, array.shape[1], width)]
 
 
 def with_halo(block, sides, width):
@@ -135,7 +257,10 @@
     local_frames = first_frame + jnp.arange(frame_rows, dtype=jnp.int32)
     local_clip = clip_of(local_frames, clip_ends)
     valid_rows = (local_frames < clip_ends[-1]).astype(jnp.float32)[:, None]
-    all_frames = jnp.arange(total_frames, dtype=jnp.int32)
+    block_order = lax.axis_index("seq") ^ jnp.arange(shard_count, dtype=jnp.int32)
+    all_frames = (
+        block_order[:, None] * frame_rows + jnp.arange(frame_rows, dtype=jnp.int32)[None, :]
+    ).reshape(total_frames)
     key_span = block_rows(frame_rows, shard_count)
     block_count = total_frames // key_span
     key_clip = clip_of(all_frames, clip_ends).reshape(block_count, key_span)
@@ -153,10 +278,13 @@
     def split_keys(array):
         return array.reshape(block_count, key_span, head_count, head_width)
 
-    projected = plain_product(input_low, w_qkv)
-    query_part = projected[:, :model_width]
-    key_low = projected[:, model_width : 2 * model_width].astype(jnp.bfloat16)
-    value_low = projected[:, 2 * model_width :].astype(jnp.bfloat16)
+    frames_all = gather_frames(input_low)
+    query_part = plain_product(input_low, w_qkv[:, :model_width])
+    pair_all = plain_product(
+        frames_all.reshape(total_frames, model_width), w_qkv[:, model_width:]
+    ).astype(jnp.bfloat16)
+    keys_all = pair_all[:, :model_width]
+    values_all = pair_all[:, model_width:]
     query_unit = (
         (query_part + rel_bias[0]).astype(jnp.bfloat16).reshape(frame_rows, head_count, head_width)
     )
@@ -166,11 +294,6 @@
     pos_grid = w_pos.reshape(model_width, head_count, head_width)
     shifted = jnp.einsum("fhd,chd->fhc", query_shift, pos_grid, preferred_element_type=jnp.float32)
     query_pos = rotate_local(shifted).astype(jnp.bfloat16)
-    keys_all, values_all = (
-        lax.all_gather(key_low, "seq", axis=0, tiled=True),
-        lax.all_gather(value_low, "seq", axis=0, tiled=True),
-    )
-
     def scores_of(key_block, table_block, clip_block):
         same_clip = local_clip[:, None] == clip_block[None, :]
         return block_scores(query_unit, query_pos, key_block, table_block, same_clip)
@@ -231,13 +354,12 @@
         convolved = convolved + conv_depth[offset] * jnp.where(
             same_clip, gated_ext[offset : offset + frame_rows].astype(jnp.float32), 0.0
         )
-    frame_count, first_moment, second_moment = lax.psum(
+    frame_count, first_moment, second_moment = sum_small(
         (
             jnp.sum(valid_rows),
             jnp.sum(convolved * valid_rows, axis=0),
             jnp.sum(convolved * convolved * valid_rows, axis=0),
-        ),
-        ("seq", "dp"),
+        )
     )
     batch_mean = first_moment / frame_count
     batch_var = second_moment / frame_count - batch_mean * batch_mean
@@ -263,17 +385,14 @@
     third_grad_low = grad_third.astype(jnp.bfloat16)
     d_conv_out = transposed_times(swished, third_grad_low)
     d_swished = times_transposed(third_grad_low, conv_out)
+    late_sums = sum_rows_everywhere(column_tiles(d_in_late, model_width) + [d_out_late, d_conv_out])
     d_normed = jax.vjp(jax.nn.silu, normed)[1](d_swished)[0]
     scaled = d_normed * bn_gain
-    d_bn_gain, d_bn_bias, sum_scaled, sum_product = lax.psum(
-        (
-            jnp.sum(d_normed * centered_conv, axis=0),
-            jnp.sum(d_normed, axis=0),
-            jnp.sum(scaled, axis=0),
-            jnp.sum(scaled * centered_conv, axis=0),
-        ),
-        ("seq", "dp"),
-    )
+    d_bn_gain, d_bn_bias = sum_small(
+        (jnp.sum(d_normed * centered_conv, axis=0), jnp.sum(d_normed, axis=0))
+    )
+    sum_scaled = d_bn_bias * bn_gain
+    sum_product = d_bn_gain * bn_gain
     d_conv = (
         inverse_std
         * (scaled - valid_rows * (sum_scaled + centered_conv * sum_product) / frame_count)
@@ -304,7 +423,6 @@
     grad_second, gain_one, bias_one = norm_back(
         second_sum, norm_gain[1], norm_bias[1], grad_third + times_transposed(d_gates, conv_in)
     )
-    late_terms = (d_in_late, d_out_late, d_conv_in, d_depth, d_conv_out)
     from_early, d_in_early, d_out_early = feed_back(
         first_low, inner_early, act_early, ffn_in[0], ffn_out[0], grad_second
     )
@@ -320,16 +438,15 @@
     )
     keys_back, values_back = (keys_all, values_all)
 
-    def delta_step(summed, pieces):
-        key_block, value_block, table_block, clip_block = pieces
-        probs = jnp.exp(scores_of(key_block, table_block, clip_block) - log_total[..., None])
-        slope = jnp.einsum(
-            "qhd,khd->hqk", d_attended, value_block, preferred_element_type=jnp.float32
-        )
-        return (summed + jnp.sum(probs * slope, axis=2), None)
-
     key_pieces = (split_keys(keys_back), split_keys(values_back), key_table, key_clip)
-    delta, _ = lax.scan(delta_step, jnp.zeros((head_count, frame_rows), jnp.float32), key_pieces)
+    delta = jnp.einsum("qhd,qhd->hq", d_attended.astype(jnp.float32), attended)
+    early_sums = sum_rows_everywhere(
+        column_tiles(d_in_early, model_width)
+        + [d_out_early]
+        + column_tiles(d_conv_in, model_width)
+        + [d_w_out]
+        + [jnp.stack([gain_zero, gain_one, gain_two, gain_three, bias_zero, bias_one, bias_two, bias_three])]
+    )
 
     def grad_step(carry, pieces):
         d_unit, d_pos = carry
@@ -359,20 +476,16 @@
         jnp.zeros((frame_rows, head_count, model_width), jnp.float32),
     )
     (d_unit, d_pos), (key_blocks, value_blocks) = lax.scan(grad_step, start_grads, key_pieces)
-    d_keys, d_values = (
-        lax.psum_scatter(
-            key_blocks.reshape(total_frames, model_width).astype(jnp.bfloat16),
-            "seq",
-            scatter_dimension=0,
-            tiled=True,
-        ).astype(jnp.float32),
-        lax.psum_scatter(
-            value_blocks.reshape(total_frames, model_width).astype(jnp.bfloat16),
-            "seq",
-            scatter_dimension=0,
-            tiled=True,
-        ).astype(jnp.float32),
-    )
+    d_pair = jnp.concatenate(
+        [
+            key_blocks.reshape(total_frames, model_width),
+            value_blocks.reshape(total_frames, model_width),
+        ],
+        axis=1,
+    ).astype(jnp.bfloat16)
+    d_frames = times_transposed(d_pair, w_qkv[:, model_width:]).astype(jnp.bfloat16)
+    from_pair = scatter_frames(d_frames.reshape(shard_count, frame_rows, model_width))
+    d_w_pair = transposed_times(frames_all.reshape(total_frames, model_width), d_pair)
     d_shifted = jax.vjp(rotate_local, shifted)[1](d_pos)[0].astype(jnp.bfloat16)
     d_w_pos = jnp.einsum(
         "fhc,fhd->chd", d_shifted, query_shift, preferred_element_type=jnp.float32
@@ -385,35 +498,22 @@
         ]
     )
     d_query = (d_unit + d_from_pos).reshape(frame_rows, model_width)
-    d_proj = jnp.concatenate([d_query, d_keys, d_values], axis=1).astype(jnp.bfloat16)
-    d_w_qkv = transposed_times(input_low, d_proj)
-    input_grad = grad_first + times_transposed(d_proj, w_qkv)
-    gain_grads = jnp.stack([gain_zero, gain_one, gain_two, gain_three])
-    bias_grads = jnp.stack([bias_zero, bias_one, bias_two, bias_three])
-    summed_all = lax.psum(
-        (
-            d_w_qkv,
-            d_w_pos,
-            d_w_out,
-            d_rel,
-            d_in_early,
-            d_out_early,
-            gain_grads,
-            bias_grads,
-            d_in_late,
-            d_out_late,
-            d_conv_in,
-            d_depth,
-            d_conv_out,
-        ),
-        ("seq", "dp"),
-    )
-    early_terms = summed_all[:8]
-    late_terms = summed_all[8:]
-    sum_qkv, sum_pos, sum_wout, sum_rel, sum_in_early, sum_out_early, sum_gain, sum_bias = (
-        early_terms
-    )
-    sum_in_late, sum_out_late, sum_conv_in, sum_depth, sum_conv_out = late_terms
+    d_query = d_query.astype(jnp.bfloat16)
+    d_w_query = transposed_times(input_low, d_query)
+    input_grad = grad_first + times_transposed(d_query, w_qkv[:, :model_width]) + from_pair
+    last_sums = sum_rows_everywhere(
+        [d_w_query] + column_tiles(d_w_pair, model_width) + [d_w_pos, d_depth, d_rel]
+    )
+    tiles = ffn_in.shape[2] // model_width
+    sum_in_late = jnp.concatenate(late_sums[:tiles], axis=1)
+    sum_out_late, sum_conv_out = late_sums[tiles:]
+    sum_in_early = jnp.concatenate(early_sums[:tiles], axis=1)
+    sum_out_early = early_sums[tiles]
+    sum_conv_in = jnp.concatenate(early_sums[tiles + 1 : tiles + 3], axis=1)
+    sum_wout, sum_norms = early_sums[tiles + 3 :]
+    sum_gain, sum_bias = sum_norms[:4], sum_norms[4:]
+    sum_qkv = jnp.concatenate(last_sums[:3], axis=1)
+    sum_pos, sum_depth, sum_rel = last_sums[3:]
     return (
         result[None],
         input_grad[None],

time: 798 us -> 583 us (0.73)
  waiting for transfers between devices: 366 us -> 92.6 us
  local copies, waits for them, and re-layouts: 75.6 us -> 208 us
  blocking collectives: 124 us -> 0 us
  starting transfers between devices: 12.1 us -> 93.1 us
  matrix products: 137 us -> 110 us
  between operations: 17.7 us -> 4.72 us
  other arithmetic: 52.3 us -> 63.6 us
    psum x1 -> x0, waiting for transfers between devices: 194 us -> none  [local(): lax.psum((d_w_qkv, d_w_pos, d_w_out, d_rel, d_in_early, d_out_early, gain...]
    psum x3 -> x0, blocking collectives: 124 us -> none  [the longest x1 42.1 us: local(): lax.psum((d_w_qkv, d_w_pos, d_w_out, d_rel, d_in_early, d_out_early, gain...]
    reduce_scatter x2 -> x0, waiting for transfers between devices: 105 us -> none  [the longest x1 63.8 us: local(): lax.psum_scatter(key_blocks.reshape(total_frames, model_width).astype(jnp...]
    ppermute x0 -> x56, waiting for transfers between devices: none -> 86.2 us  [the longest x42 65.7 us: swap_flat(): return lax.ppermute(block, MODEL_AXES, pairs)]
    ppermute x0 -> x56, starting transfers between devices: none -> 71.9 us  [the longest x42 52.9 us: swap_flat(): return lax.ppermute(block, MODEL_AXES, pairs)]
    all_gather x2 -> x0, waiting for transfers between devices: 60.5 us -> none  [the longest x1 39.2 us: local(): lax.all_gather(key_low, 'seq', axis=0, tiled=True)]
    dynamic_update_slice x0 -> x29, local copies, waits for them, and re-layouts: none -> 37.4 us  [sum_everywhere(): lax.dynamic_update_index_in_dim(gathered, arrived[step], digit ^ step, 0)]
    concatenate x0 -> x7, local copies, waits for them, and re-layouts: none -> 26.2 us  [the longest x5 22.1 us: sum_rows_everywhere(): jnp.concatenate([part.astype(jnp.bfloat16) for part in parts] + [padding]...]
  transfers between devices with their start and end apart: 9 -> 62, of which waited for: 7 -> 29; matrix products, arithmetic and copies ran while one was open for 7% -> 45% of each run, Pallas kernels for 0% -> 0%
where the time goes in v1:
time: 583 us; the launch traced here: 573 us
  local copies, waits for them, and re-layouts  208 us (36%)
  matrix products  110 us (19%)
  starting transfers between devices  93.1 us (16%)
  waiting for transfers between devices  92.6 us (16%)
  other arithmetic  63.6 us (11%)
    ppermute x42, waiting for transfers between devices, swap_flat(): return lax.ppermute(block, MODEL_AXES, pairs)  65.7 us
    ppermute x42, starting transfers between devices, swap_flat(): return lax.ppermute(block, MODEL_AXES, pairs)  52.9 us
    dynamic_update_slice x29, local copies, waits for them, and re-layouts, sum_everywhere(): lax.dynamic_update_index_in_dim(gathered, arrived[step], digit ^ step, 0)  37.4 us
    unnamed x436, local copies, waits for them, and re-layouts  36.3 us
    another operation x31, local copies, waits for them, and re-layouts, local(): d_depth = jnp.stack(depth_terms)  22.4 us
    concatenate x5, local copies, waits for them, and re-layouts, sum_rows_everywhere(): jnp.concatenate([part.astype(jnp.bfloat16) for part in parts] + [padding]...  22.1 us
    ppermute x14, waiting for transfers between devices, swap_seq(): return lax.ppermute(block, 'seq', pairs)  20.5 us
    ppermute x14, starting transfers between devices, swap_seq(): return lax.ppermute(block, 'seq', pairs)  19 us
  transfers between devices with their start and end apart: 62, of which 29 were waited for; matrix products, arithmetic and copies ran while one was open for 45% of the time, Pallas kernels for 0%

profile of v1, /device:TPU:0, one launch (start us, length us, event | category | flops | bytes accessed | tf_op | source)
XLA Modules:
  0.0 573.3 jit_solution(11869502223673590738)
XLA Ops:
  15.8 7.2 %fusion.247 = (bf16[1,1296,324]{1,0,2:T(2,128)(2,1)}, bf16[1,1296,324]{1,0,2:T(2,128)(2,1)}) fusion(bf16[2,1296,324]{1,0,2:T(2,128)(2,1)} %param.28), kind=kLoop, calls=%fused_computation.710 | loop fusion | bytes 3359232 | tf_op jit(solution)/shard_map/slice | solution.py:340
  23.0 4.3 fusion.246
  29.9 5.7 fusion.66
  58.7 4.1 reshape.607
  70.1 15.4 %while.41 = (s32[]{:T(128)}, f32[4,256]{1,0:T(4,128)S(1)}, f32[4,256]{1,0:T(4,128)S(1)}, s32[256]{0:T(256)S(1)}, s32[4,512]{1,0:T(4,128)S(1)}, /*index=5*/bf16[4...) while((s32[]{:T(128)}, f32[4,256]{1,0:T(4,128)S(1)}, ...), condition=%wide.region_6.7_spmd.clone, body=%wide.region_3.6_spmd.clone.sunk | while | flops 427955200 | bytes 10237068 | solution.py:315
  85.6 22.4 %while.42 = (s32[]{:T(128)}, f32[256,4,81]{0,2,1:T(8,128)}, bf16[4,512,4,81]{1,3,2,0:T(8,128)(2,1)}, s32[256]{0:T(256)S(1)}, s32[4,512]{1,0:T(4,128)S(1)}, /*ind...) while((s32[]{:T(128)}, f32[256,4,81]{0,2,1:T(8,128)}, ...), condition=%wide.region_8.9_spmd.clone, body=%wide.region_7.8_spmd.clone.sunk | while | flops 512526336 | bytes 7047822 | solution.py:331
  116.7 4.6 collective-permute-start.7
  123.6 7.0 %multiply_reduce_fusion.11 = (f32[324]{0:T(512)S(1)}, f32[324]{0:T(512)S(1)}, f32[256,324]{0,1:T(8,128)}) fusion(f32[256]{0:T(256)S(1)} %compare_convert_fusion, bf16[15,324]{0,1:T(8,128)(2,1)S(1)} %collective-permute-done.8, bf16[256,324]{0,1:T(8,128)(2,1)S(1)} %multiply_convert_fusion.4, pred[256]{0:T(512)(128)(4,1)S(1)} %copy-done.177, ...), kind=kLoop, calls=%fused_computation.399 | loop fusion | flops 18081144 | bytes 568832 | tf_op jit(solution)/shard_map/reduce_sum | solution.py:360
  132.1 6.8 %all-to-all-start = ((f32[32,8,128]{2,1,0:T(8,128)}), f32[32,8,128]{2,1,0:T(8,128)S(1)}, u32[]{:S(2)}, u32[]{:S(2)}) async-start(f32[32,8,128]{2,1,0:T(8,128)} %broadcast_in_dim.814), calls=%async_computation | async-start | bytes 262144 | tf_op jit(solution)/shard_map/all_to_all | solution.py:96
  140.8 6.2 %all-to-all-done = f32[32,8,128]{2,1,0:T(8,128)S(1)} async-done(((f32[32,8,128]{2,1,0:T(8,128)}), f32[32,8,128]{2,1,0:T(8,128)S(1)}, u32[]{:S(2)}, u32[]{:S(2)}) %all-to-all-start) | async-done | bytes 131104 | tf_op jit(solution)/shard_map/all_to_all | solution.py:96
  177.0 5.1 concatenate.134
  182.1 4.1 copy.304
  193.3 3.6 collective-permute-start.10
  227.8 6.0 %fusion.93 = (f32[256,324]{0,1:T(8,128)S(1)}, f32[256,324]{0,1:T(8,128)S(1)}) fusion(f32[256,648]{0,1:T(8,128)S(1)} %fusion.231, bf16[256,324]{0,1:T(8,128)(2,1)S(1)} %get-tuple-element.668, bf16[15,324]{0,1:T(8,128)(2,1)S(1)} %collective-permute-done.10, pred[256]{0:T(512)(128)(4,1)S(1)} %copy-done.176, f32[324]{0:T(512)S(1)} %copy-done.156, ...), kind=kLoop, calls=%fused_computation.321 | loop fusion | flops 18247680 | bytes 1560544 | tf_op jit(solution)/shard_map/transpose(jvp())/mul | solution.py:197
  241.7 57.9 %while.43 = (s32[]{:T(128)}, f32[256,4,81]{0,2,1:T(8,128)}, f32[256,4,324]{0,2,1:T(8,128)}, bf16[4,512,4,81]{1,3,2,0:T(8,128)(2,1)}, bf16[4,512,4,81]{1,3,2,0:T(...) while((s32[]{:T(128)}, f32[256,4,81]{0,2,1:T(8,128)}, ...), condition=%wide.region_34.35_spmd.clone, body=%wide.region_33.34_spmd.clone.sunk | while | flops 1109829632 | bytes 60014000 | solution.py:478
  325.5 5.7 concatenate.129
  336.7 6.4 %concatenate.132 = bf16[3584,324]{0,1:T(8,128)(2,1)} concatenate(bf16[324,324]{0,1:T(8,128)(2,1)S(1)} %copy.282, bf16[324,324]{0,1:T(8,128)(2,1)S(1)} %copy.283, bf16[324,324]{0,1:T(8,128)(2,1)S(1)} %copy.284, bf16[324,324]{0,1:T(8,128)(2,1)S(1)} %copy.285, bf16[1296,324]{0,1:T(8,128)(2,1)} %convolution_convert_fusion.3, bf16[324,324]{0,1:T(8,128)(2,1)S(1)} %get-tuple-element.737, ...), dimensions={0} | concatenate | bytes 4644864 | tf_op jit(solution)/shard_map/concatenate | solution.py:80
  343.1 5.3 reshape_reshape.20
  357.8 4.7 collective-permute-done.20
  384.2 7.4 %collective-permute-done.14 = bf16[256,324]{0,1:T(8,128)(2,1)S(1)} collective-permute-done((bf16[256,324]{0,1:T(8,128)(2,1)S(1)}, bf16[256,324]{0,1:T(8,128)(2,1)S(1)}, u32[]{:S(2)}, u32[]{:S(2)}) %collective-permute-start.14) | collective-permute-done | bytes 165920 | tf_op jit(solution)/shard_map/ppermute | solution.py:28
  412.6 3.6 collective-permute-done.49
  416.2 6.7 %collective-permute-done.48 = bf16[4,96,324]{2,1,0:T(8,128)(2,1)S(1)} collective-permute-done((bf16[4,96,324]{2,1,0:T(8,128)(2,1)S(1)}, bf16[4,96,324]{2,1,0:T(8,128)(2,1)S(1)}, u32[]{:S(2)}, u32[]{:S(2)}) %collective-permute-start.48) | collective-permute-done | bytes 248864 | tf_op jit(solution)/shard_map/ppermute | solution.py:23
  428.6 4.1 collective-permute-done.50
  459.0 9.4 %collective-permute-done.34 = bf16[4,112,324]{1,0,2:T(4,128)(2,1)S(1)} collective-permute-done((bf16[4,112,324]{1,0,2:T(4,128)(2,1)S(1)}, bf16[4,112,324]{1,0,2:T(4,128)(2,1)S(1)}, u32[]{:S(2)}, u32[]{:S(2)}) %collective-permute-start.34) | collective-permute-done | bytes 290336 | tf_op jit(solution)/shard_map/ppermute | solution.py:23
  477.2 6.1 %collective-permute-done.37 = bf16[1,112,324]{1,0,2:T(2,128)(2,1)S(1)} collective-permute-done((bf16[1,112,324]{1,0,2:T(2,128)(2,1)S(1)}, bf16[1,112,324]{1,0,2:T(2,128)(2,1)S(1)}, u32[]{:S(2)}, u32[]{:S(2)}) %collective-permute-start.37) | collective-permute-done | bytes 72608 | tf_op jit(solution)/shard_map/ppermute | solution.py:23
  489.8 4.6 dynamic_update_slice.128
  494.4 4.6 dynamic_update_slice.129
  499.1 4.6 dynamic_update_slice.130
  503.7 4.9 dynamic_update_slice.131
  520.2 9.1 %collective-permute-done.43 = bf16[4,112,324]{1,0,2:T(4,128)(2,1)S(1)} collective-permute-done((bf16[4,112,324]{1,0,2:T(4,128)(2,1)S(1)}, bf16[4,112,324]{1,0,2:T(4,128)(2,1)S(1)}, u32[]{:S(2)}, u32[]{:S(2)}) %collective-permute-start.43) | collective-permute-done | bytes 290336 | tf_op jit(solution)/shard_map/ppermute | solution.py:23
  557.2 3.7 copy.307
  563.2 7.6 %copy.308 = f32[2,1296,324]{1,0,2:T(2,128)} copy(f32[2,1296,324]{2,1,0:T(8,128)} %maximum_convert_fusion) | data formatting | bytes 6718464
  (948 shorter events, 403.8 us)
Async XLA Ops:
  0.7 42.7 %collective-permute-start = (bf16[256,324]{0,1:T(8,128)(2,1)}, bf16[256,324]{0,1:T(8,128)(2,1)}, u32[]{:S(2)}, u32[]{:S(2)}) collective-permute-start(bf16[256,324]{0,1:T(8,128)(2,1)} %bitcast.478), channel_id=1, source_target_pairs={{0,4},{4,0},{8,12},{12,8},{16,20},{20,16},{24,28},{28,24},{1,5},{5... | collective-permute-start | bytes 497672 | tf_op jit(solution)/shard_map/ppermute | solution.py:28
  3.7 37.3 %collective-permute-start.1 = (bf16[256,324]{0,1:T(8,128)(2,1)}, bf16[256,324]{0,1:T(8,128)(2,1)}, u32[]{:S(2)}, u32[]{:S(2)}) collective-permute-start(bf16[256,324]{0,1:T(8,128)(2,1)} %bitcast.479), channel_id=1, source_target_pairs={{0,8},{4,12},{8,0},{12,4},{16,24},{20,28},{24,16},{28,20},{1,9},{5... | collective-permute-start | bytes 497672 | tf_op jit(solution)/shard_map/ppermute | solution.py:28
  5.3 36.1 %collective-permute-start.3 = (bf16[256,324]{0,1:T(8,128)(2,1)}, bf16[256,324]{0,1:T(8,128)(2,1)}, u32[]{:S(2)}, u32[]{:S(2)}) collective-permute-start(bf16[256,324]{0,1:T(8,128)(2,1)} %bitcast.480), channel_id=1, source_target_pairs={{0,16},{4,20},{8,24},{12,28},{16,0},{20,4},{24,8},{28,12},{1,17},{... | collective-permute-start | bytes 497672 | tf_op jit(solution)/shard_map/ppermute | solution.py:28
  7.9 35.2 %collective-permute-start.5 = (bf16[256,324]{0,1:T(8,128)(2,1)}, bf16[256,324]{0,1:T(8,128)(2,1)}, u32[]{:S(2)}, u32[]{:S(2)}) collective-permute-start(bf16[256,324]{0,1:T(8,128)(2,1)} %bitcast.481), channel_id=1, source_target_pairs={{0,24},{4,28},{8,16},{12,20},{16,8},{20,12},{24,0},{28,4},{1,25},{... | collective-permute-start | bytes 497672 | tf_op jit(solution)/shard_map/ppermute | solution.py:28
  132.1 15.0 %all-to-all-start = ((f32[32,8,128]{2,1,0:T(8,128)}), f32[32,8,128]{2,1,0:T(8,128)S(1)}, u32[]{:S(2)}, u32[]{:S(2)}) async-start(f32[32,8,128]{2,1,0:T(8,128)} %broadcast_in_dim.814), calls=%async_computation | async-start | bytes 262144 | tf_op jit(solution)/shard_map/all_to_all | solution.py:96
  160.4 28.4 %all-to-all-start.1 = ((f32[32,8,128]{2,1,0:T(8,128)}), f32[32,8,128]{2,1,0:T(8,128)}, u32[]{:S(2)}, u32[]{:S(2)}) async-start(f32[32,8,128]{2,1,0:T(8,128)} %broadcast_in_dim.821), calls=%async_computation.1 | async-start | bytes 262144 | tf_op jit(solution)/shard_map/all_to_all | solution.py:96
  188.8 215.7 %collective-permute-start.46 = (bf16[16,96,324]{2,1,0:T(8,128)(2,1)}, bf16[16,96,324]{2,1,0:T(8,128)(2,1)}, u32[]{:S(2)}, u32[]{:S(2)}) collective-permute-start(bf16[16,96,324]{2,1,0:T(8,128)(2,1)} %dynamic-slice_bitcast_fusion.1), channel_id=1, source_target_pairs={{0,1},{1,0},{2,3},{3,2},{4,5},{5,4},{6,7},{7,6},{8,9},{9,8},{10,11... | collective-permute-start | bytes 2985992 | tf_op jit(solution)/shard_map/ppermute | solution.py:23
  193.3 34.2 %collective-permute-start.10 = (bf16[15,324]{0,1:T(8,128)(2,1)S(1)}, bf16[15,324]{0,1:T(8,128)(2,1)S(1)}, u32[]{:S(2)}, u32[]{:S(2)}) collective-permute-start(bf16[15,324]{0,1:T(8,128)(2,1)S(1)} %get-tuple-element.753), channel_id=1, source_target_pairs={{0,4},{4,8},{8,12},{12,16},{16,20},{20,24},{24,28},{1,5},{5,9},{9,... | collective-permute-start | bytes 29168 | tf_op jit(solution)/shard_map/ppermute | solution.py:138
  196.9 30.6 %collective-permute-start.9 = (bf16[15,324]{0,1:T(8,128)(2,1)S(1)}, bf16[15,324]{0,1:T(8,128)(2,1)S(1)}, u32[]{:S(2)}, u32[]{:S(2)}) collective-permute-start(bf16[15,324]{0,1:T(8,128)(2,1)S(1)} %get-tuple-element.752), channel_id=1, source_target_pairs={{4,0},{8,4},{12,8},{16,12},{20,16},{24,20},{28,24},{5,1},{9,5},{13... | collective-permute-start | bytes 29168 | tf_op jit(solution)/shard_map/ppermute | solution.py:141
  319.7 62.6 %collective-permute-start.17 = (bf16[256,324]{0,1:T(8,128)(2,1)}, bf16[256,324]{0,1:T(8,128)(2,1)}, u32[]{:S(2)}, u32[]{:S(2)}) collective-permute-start(bf16[256,324]{0,1:T(8,128)(2,1)} %get-tuple-element.712), channel_id=1, source_target_pairs={{0,4},{4,0},{8,12},{12,8},{16,20},{20,16},{24,28},{28,24},{1,5},{5... | collective-permute-start | bytes 497672 | tf_op jit(solution)/shard_map/ppermute | solution.py:28
  332.9 16.7 %collective-permute-start.18 = (bf16[16,48,324]{2,1,0:T(8,128)(2,1)}, bf16[16,48,324]{2,1,0:T(8,128)(2,1)}, u32[]{:S(2)}, u32[]{:S(2)}) collective-permute-start(bf16[16,48,324]{2,1,0:T(8,128)(2,1)} %dynamic-slice_bitcast_fusion.2), channel_id=1, source_target_pairs={{0,1},{1,0},{2,3},{3,2},{4,5},{5,4},{6,7},{7,6},{8,9},{9,8},{10,11... | collective-permute-start | bytes 1493000 | tf_op jit(solution)/shard_map/ppermute | solution.py:23
  376.3 15.3 %collective-permute-start.14 = (bf16[256,324]{0,1:T(8,128)(2,1)S(1)}, bf16[256,324]{0,1:T(8,128)(2,1)S(1)}, u32[]{:S(2)}, u32[]{:S(2)}) collective-permute-start(bf16[256,324]{0,1:T(8,128)(2,1)S(1)} %get-tuple-element.710), channel_id=1, source_target_pairs={{0,16},{4,20},{8,24},{12,28},{16,0},{20,4},{24,8},{28,12},{1,17},{... | collective-permute-start | bytes 497672 | tf_op jit(solution)/shard_map/ppermute | solution.py:28
  378.7 13.0 %collective-permute-start.12 = (bf16[256,324]{0,1:T(8,128)(2,1)S(1)}, bf16[256,324]{0,1:T(8,128)(2,1)S(1)}, u32[]{:S(2)}, u32[]{:S(2)}) collective-permute-start(bf16[256,324]{0,1:T(8,128)(2,1)S(1)} %get-tuple-element.708), channel_id=1, source_target_pairs={{0,24},{4,28},{8,16},{12,20},{16,8},{20,12},{24,0},{28,4},{1,25},{... | collective-permute-start | bytes 497672 | tf_op jit(solution)/shard_map/ppermute | solution.py:28
  382.3 65.0 %collective-permute-start.32 = (bf16[16,112,324]{1,0,2:T(8,128)(2,1)S(1)}, bf16[16,112,324]{1,0,2:T(8,128)(2,1)S(1)}, u32[]{:S(2)}, u32[]{:S(2)}) collective-permute-start(bf16[16,112,324]{1,0,2:T(8,128)(2,1)S(1)} %dynamic-slice_bitcast_fusion), channel_id=1, source_target_pairs={{0,1},{1,0},{2,3},{3,2},{4,5},{5,4},{6,7},{7,6},{8,9},{9,8},{10,11... | collective-permute-start | bytes 3483656 | tf_op jit(solution)/shard_map/ppermute | solution.py:23
  384.2 14.9 %collective-permute-start.25 = (bf16[1,48,324]{2,1,0:T(8,128)(2,1)S(1)}, bf16[1,48,324]{2,1,0:T(8,128)(2,1)S(1)}, u32[]{:S(2)}, u32[]{:S(2)}) collective-permute-start(bf16[1,48,324]{2,1,0:T(8,128)(2,1)S(1)} %get-tuple-element.667), channel_id=1, source_target_pairs={{0,8},{1,9},{2,10},{3,11},{4,12},{5,13},{6,14},{7,15},{8,0},{9,1},... | collective-permute-start | bytes 93320 | tf_op jit(solution)/shard_map/ppermute | solution.py:23
  407.6 15.2 %collective-permute-start.48 = (bf16[4,96,324]{2,1,0:T(8,128)(2,1)S(1)}, bf16[4,96,324]{2,1,0:T(8,128)(2,1)S(1)}, u32[]{:S(2)}, u32[]{:S(2)}) collective-permute-start(bf16[4,96,324]{2,1,0:T(8,128)(2,1)S(1)} %get-tuple-element.720), channel_id=1, source_target_pairs={{0,4},{1,5},{2,6},{3,7},{4,0},{5,1},{6,2},{7,3},{8,12},{9,13},{10,... | collective-permute-start | bytes 746504 | tf_op jit(solution)/shard_map/ppermute | solution.py:23
  409.5 13.3 %collective-permute-start.47 = (bf16[4,96,324]{2,1,0:T(8,128)(2,1)S(1)}, bf16[4,96,324]{2,1,0:T(8,128)(2,1)S(1)}, u32[]{:S(2)}, u32[]{:S(2)}) collective-permute-start(bf16[4,96,324]{2,1,0:T(8,128)(2,1)S(1)} %get-tuple-element.718), channel_id=1, source_target_pairs={{0,6},{1,7},{2,4},{3,5},{4,2},{5,3},{6,0},{7,1},{8,14},{9,15},{10,... | collective-permute-start | bytes 746504 | tf_op jit(solution)/shard_map/ppermute | solution.py:23
  410.7 16.8 %collective-permute-start.30 = (bf16[4,48,324]{2,1,0:T(8,128)(2,1)S(1)}, bf16[4,48,324]{2,1,0:T(8,128)(2,1)S(1)}, u32[]{:S(2)}, u32[]{:S(2)}) collective-permute-start(bf16[4,48,324]{2,1,0:T(8,128)(2,1)S(1)} %constant_dynamic-update-slice_fusion.7), channel_id=1, source_target_pairs={{0,6},{1,7},{2,4},{3,5},{4,2},{5,3},{6,0},{7,1},{8,14},{9,15},{10,... | collective-permute-start | bytes 373256 | tf_op jit(solution)/shard_map/ppermute | solution.py:23
  427.5 21.3 %collective-permute-start.31 = (bf16[16,48,324]{2,1,0:T(8,128)(2,1)S(1)}, bf16[16,48,324]{2,1,0:T(8,128)(2,1)S(1)}, u32[]{:S(2)}, u32[]{:S(2)}) collective-permute-start(bf16[16,48,324]{2,1,0:T(8,128)(2,1)S(1)} %bitcast.474), channel_id=1, source_target_pairs={{0,1},{1,0},{2,3},{3,2},{4,5},{5,4},{6,7},{7,6},{8,9},{9,8},{10,11... | collective-permute-start | bytes 1493000 | tf_op jit(solution)/shard_map/ppermute | solution.py:23
  441.6 13.6 %collective-permute-start.56 = (bf16[4,96,324]{2,1,0:T(8,128)(2,1)S(1)}, bf16[4,96,324]{2,1,0:T(8,128)(2,1)S(1)}, u32[]{:S(2)}, u32[]{:S(2)}) collective-permute-start(bf16[4,96,324]{2,1,0:T(8,128)(2,1)S(1)} %constant_dynamic-update-slice_fusion.1), channel_id=1, source_target_pairs={{0,2},{1,3},{2,0},{3,1},{4,6},{5,7},{6,4},{7,5},{8,10},{9,11},{10,... | collective-permute-start | bytes 746504 | tf_op jit(solution)/shard_map/ppermute | solution.py:23
  444.0 29.7 %collective-permute-start.57 = (bf16[4,96,324]{2,1,0:T(8,128)(2,1)S(1)}, bf16[4,96,324]{2,1,0:T(8,128)(2,1)S(1)}, u32[]{:S(2)}, u32[]{:S(2)}) collective-permute-start(bf16[4,96,324]{2,1,0:T(8,128)(2,1)S(1)} %constant_dynamic-update-slice_fusion.1), channel_id=1, source_target_pairs={{0,4},{1,5},{2,6},{3,7},{4,0},{5,1},{6,2},{7,3},{8,12},{9,13},{10,... | collective-permute-start | bytes 746504 | tf_op jit(solution)/shard_map/ppermute | solution.py:23
  448.8 19.6 %collective-permute-start.34 = (bf16[4,112,324]{1,0,2:T(4,128)(2,1)S(1)}, bf16[4,112,324]{1,0,2:T(4,128)(2,1)S(1)}, u32[]{:S(2)}, u32[]{:S(2)}) collective-permute-start(bf16[4,112,324]{1,0,2:T(4,128)(2,1)S(1)} %get-tuple-element.717), channel_id=1, source_target_pairs={{0,4},{1,5},{2,6},{3,7},{4,0},{5,1},{6,2},{7,3},{8,12},{9,13},{10,... | collective-permute-start | bytes 870920 | tf_op jit(solution)/shard_map/ppermute | solution.py:23
  448.8 19.6 %collective-permute-start.33 = (bf16[4,112,324]{1,0,2:T(4,128)(2,1)S(1)}, bf16[4,112,324]{1,0,2:T(4,128)(2,1)S(1)}, u32[]{:S(2)}, u32[]{:S(2)}) collective-permute-start(bf16[4,112,324]{1,0,2:T(4,128)(2,1)S(1)} %get-tuple-element.715), channel_id=1, source_target_pairs={{0,6},{1,7},{2,4},{3,5},{4,2},{5,3},{6,0},{7,1},{8,14},{9,15},{10,... | collective-permute-start | bytes 870920 | tf_op jit(solution)/shard_map/ppermute | solution.py:23
  455.2 33.7 %collective-permute-start.58 = (bf16[4,96,324]{2,1,0:T(8,128)(2,1)S(1)}, bf16[4,96,324]{2,1,0:T(8,128)(2,1)S(1)}, u32[]{:S(2)}, u32[]{:S(2)}) collective-permute-start(bf16[4,96,324]{2,1,0:T(8,128)(2,1)S(1)} %constant_dynamic-update-slice_fusion.1), channel_id=1, source_target_pairs={{0,6},{1,7},{2,4},{3,5},{4,2},{5,3},{6,0},{7,1},{8,14},{9,15},{10,... | collective-permute-start | bytes 746504 | tf_op jit(solution)/shard_map/ppermute | solution.py:23
  469.4 14.0 %collective-permute-start.37 = (bf16[1,112,324]{1,0,2:T(2,128)(2,1)S(1)}, bf16[1,112,324]{1,0,2:T(2,128)(2,1)S(1)}, u32[]{:S(2)}, u32[]{:S(2)}) collective-permute-start(bf16[1,112,324]{1,0,2:T(2,128)(2,1)S(1)} %get-tuple-element.748), channel_id=1, source_target_pairs={{0,16},{1,17},{2,18},{3,19},{4,20},{5,21},{6,22},{7,23},{8,24},{9,... | collective-permute-start | bytes 217736 | tf_op jit(solution)/shard_map/ppermute | solution.py:23
  471.6 11.8 %collective-permute-start.36 = (bf16[1,112,324]{1,0,2:T(2,128)(2,1)S(1)}, bf16[1,112,324]{1,0,2:T(2,128)(2,1)S(1)}, u32[]{:S(2)}, u32[]{:S(2)}) collective-permute-start(bf16[1,112,324]{1,0,2:T(2,128)(2,1)S(1)} %get-tuple-element.746), channel_id=1, source_target_pairs={{0,24},{1,25},{2,26},{3,27},{4,28},{5,29},{6,30},{7,31},{8,16},{9,... | collective-permute-start | bytes 217736 | tf_op jit(solution)/shard_map/ppermute | solution.py:23
  486.5 12.6 %collective-permute-start.40 = (bf16[1,112,324]{1,0,2:T(2,128)(2,1)S(1)}, bf16[1,112,324]{1,0,2:T(2,128)(2,1)S(1)}, u32[]{:S(2)}, u32[]{:S(2)}) collective-permute-start(bf16[1,112,324]{1,0,2:T(2,128)(2,1)S(1)} %add_convert_fusion.13), channel_id=1, source_target_pairs={{0,16},{1,17},{2,18},{3,19},{4,20},{5,21},{6,22},{7,23},{8,24},{9,... | collective-permute-start | bytes 217736 | tf_op jit(solution)/shard_map/ppermute | solution.py:23
  486.8 17.0 %collective-permute-start.41 = (bf16[1,112,324]{1,0,2:T(2,128)(2,1)S(1)}, bf16[1,112,324]{1,0,2:T(2,128)(2,1)S(1)}, u32[]{:S(2)}, u32[]{:S(2)}) collective-permute-start(bf16[1,112,324]{1,0,2:T(2,128)(2,1)S(1)} %add_convert_fusion.13), channel_id=1, source_target_pairs={{0,24},{1,25},{2,26},{3,27},{4,28},{5,29},{6,30},{7,31},{8,16},{9,... | collective-permute-start | bytes 217736 | tf_op jit(solution)/shard_map/ppermute | solution.py:23
  489.7 49.5 %collective-permute-start.59 = (bf16[16,96,324]{2,1,0:T(8,128)(2,1)}, bf16[16,96,324]{2,1,0:T(8,128)(2,1)}, u32[]{:S(2)}, u32[]{:S(2)}) collective-permute-start(bf16[16,96,324]{2,1,0:T(8,128)(2,1)} %bitcast.77), channel_id=1, source_target_pairs={{0,1},{1,0},{2,3},{3,2},{4,5},{5,4},{6,7},{7,6},{8,9},{9,8},{10,11... | collective-permute-start | bytes 2985992 | tf_op jit(solution)/shard_map/ppermute | solution.py:23
  512.2 17.1 %collective-permute-start.43 = (bf16[4,112,324]{1,0,2:T(4,128)(2,1)S(1)}, bf16[4,112,324]{1,0,2:T(4,128)(2,1)S(1)}, u32[]{:S(2)}, u32[]{:S(2)}) collective-permute-start(bf16[4,112,324]{1,0,2:T(4,128)(2,1)S(1)} %dynamic_update_slice.131), channel_id=1, source_target_pairs={{0,4},{1,5},{2,6},{3,7},{4,0},{5,1},{6,2},{7,3},{8,12},{9,13},{10,... | collective-permute-start | bytes 870920 | tf_op jit(solution)/shard_map/ppermute | solution.py:23
  513.6 16.6 %collective-permute-start.44 = (bf16[4,112,324]{1,0,2:T(4,128)(2,1)S(1)}, bf16[4,112,324]{1,0,2:T(4,128)(2,1)S(1)}, u32[]{:S(2)}, u32[]{:S(2)}) collective-permute-start(bf16[4,112,324]{1,0,2:T(4,128)(2,1)S(1)} %dynamic_update_slice.131), channel_id=1, source_target_pairs={{0,6},{1,7},{2,4},{3,5},{4,2},{5,3},{6,0},{7,1},{8,14},{9,15},{10,... | collective-permute-start | bytes 870920 | tf_op jit(solution)/shard_map/ppermute | solution.py:23
  531.1 17.3 %collective-permute-start.45 = (bf16[16,112,324]{1,0,2:T(8,128)(2,1)}, bf16[16,112,324]{1,0,2:T(8,128)(2,1)}, u32[]{:S(2)}, u32[]{:S(2)}) collective-permute-start(bf16[16,112,324]{1,0,2:T(8,128)(2,1)} %bitcast.60), channel_id=1, source_target_pairs={{0,1},{1,0},{2,3},{3,2},{4,5},{5,4},{6,7},{7,6},{8,9},{9,8},{10,11... | collective-permute-start | bytes 3483656 | tf_op jit(solution)/shard_map/ppermute | solution.py:23
  (268 other events, 2887.5 us)
